TPU v7x, 256 devices: a whole 4x4x8 slice. The times are simulated.
256 devices in a mesh: row: 8 (over z), col: 32 (over y, x, core).
Axes of the slice: x: 4, y: 4, z: 8, core: 2. Of those that a mesh axis runs over, the one named last changes fastest.
Arguments:
- out_grads: bfloat16 [32, 48, 28672], P('col', None, 'row'), may hold values from -6 to 6
- acts: bfloat16 [32, 48, 8192], P('row', None, 'col'), may hold values from -6 to 6
- rot_out: bfloat16 [28672, 28672], P('row', 'col'), may hold values from -0.03125 to 0.03125
- rot_in: bfloat16 [8192, 8192], P('col', 'row'), may hold values from -0.0625 to 0.0625
- queries: bfloat16 [2, 28672, 8192], P(None, 'col', 'row'), may hold values from -0.00036621094 to 0.00036621094
- token_sequence: int32 [1024], replicated, may hold values from 0 to 31, never falling along the last dimension, each value on 1 to 48 neighbouring positions
Outputs:
- scores: float32 [1024, 2], P(('row', 'col'))
Inputs may be any that keep to these rules, and one draw needn't show every extreme that they name: `token_sequence`: values never fall along the tokens; every sequence 0 to 31 has 1 to 48 tokens, some sequence exactly 48; the k-th token of a sequence (from 0) sits in its slot k of out_grads and acts.
All inputs are finite; a program needn't handle non-finite values.
Results may differ from a plain program's by a relative error of at most 0.0041.
Values may be sent and summed in bfloat16 or wider, within the bound.
A program may use at most 128 MiB of HBM per device.

v0:
```python
import jax
import jax.numpy as jnp
from jax import lax
from jax.sharding import Mesh
from jax.sharding import PartitionSpec as P

COL = ("col_0", "col_1", "col_2")
ROW_COL = ("row", "col_0", "col_1", "col_2")


def copy_for_each(shard, axis):
    copies = jnp.broadcast_to(shard, (lax.axis_size(axis), *shard.shape))
    return lax.all_to_all(copies, axis, split_axis=0, concat_axis=0, tiled=True)


def laid_out(blocks, dim):
    lengths = list(blocks.shape[1:])
    lengths[dim] *= blocks.shape[0]
    return jnp.moveaxis(blocks, 0, dim).reshape(lengths)


def gathered_copies(shard, axis, dim):
    blocks = copy_for_each(shard, axis)
    return laid_out(blocks, dim)


def in_blocks(shard, dim, devices):
    lengths = shard.shape
    blocks = shard.reshape(*lengths[:dim], devices, lengths[dim] // devices, *lengths[dim + 1 :])
    return jnp.moveaxis(blocks, dim, 0)


def summed_on_arrival(shard, axis, dim):
    devices = lax.axis_size(axis)
    blocks = lax.all_to_all(in_blocks(shard, dim, devices), axis, 0, 0, tiled=True)
    return jnp.sum(blocks, axis=0)


def sum_by_chip_2(shard, chips, core, dim):
    sizes = (lax.axis_size(chips), lax.axis_size(core))
    blocks = in_blocks(shard, dim, sizes[0] * sizes[1])
    inside = blocks.shape[1:]
    blocks = blocks.reshape(*sizes, *inside).swapaxes(0, 1).reshape(-1, *inside)
    blocks = lax.psum_scatter(blocks, core, scatter_dimension=0, tiled=True)
    return lax.psum_scatter(blocks, chips, scatter_dimension=0, tiled=True)[0]


def token_places(token_sequence, seq_count, slot_count):
    token_count = token_sequence.shape[0]
    labels = jnp.arange(seq_count, dtype=jnp.int32)
    before = (token_sequence[:, None] < labels[None, :]).astype(jnp.int32)
    starts = jnp.sum(before, axis=0)
    member = (token_sequence[:, None] == labels[None, :]).astype(jnp.int32)
    own_start = jnp.sum(member * starts[None, :], axis=1)
    position = jnp.arange(token_count, dtype=jnp.int32) - own_start
    return token_sequence * slot_count + position


def local(out_grads, acts, rot_out, rot_in, queries, token_sequence):
    slot_count = out_grads.shape[1]
    seq_count = out_grads.shape[0] * lax.axis_size(COL)
    flat_index = token_places(token_sequence, seq_count, slot_count)
    act_slots = gathered_copies(acts, "row", 0)
    act_rows = jnp.take(
        act_slots.reshape(seq_count * slot_count, act_slots.shape[2]), flat_index, axis=0
    )
    piece = lax.all_gather(out_grads, COL, axis=0, tiled=True)
    flattened = piece.reshape(piece.shape[0] * piece.shape[1], piece.shape[2])
    slot_terms = jnp.dot(flattened, rot_out, preferred_element_type=jnp.float32)
    grad_terms = jnp.take(slot_terms, flat_index, axis=0)
    grad_share = summed_on_arrival(grad_terms, "row", 0).astype(jnp.bfloat16)
    rot_grads = gathered_copies(grad_share, "row", 0)
    act_share = sum_by_chip_2(
        jnp.dot(act_rows, rot_in, preferred_element_type=jnp.float32),
        ("col_0", "col_1"),
        "col_2",
        0,
    ).astype(jnp.bfloat16)
    rot_acts = gathered_copies(act_share, COL, 0)
    projected = jnp.einsum("tj,qij->tqi", rot_acts, queries, preferred_element_type=jnp.float32)
    score_terms = jnp.sum(projected * rot_grads[:, None, :], axis=2)
    return lax.psum_scatter(score_terms, ROW_COL, scatter_dimension=0, tiled=True)


def solution(mesh):
    torus = Mesh(
        mesh.devices.reshape(mesh.shape["row"], 4, 4, 2), ("row", "col_0", "col_1", "col_2")
    )
    in_specs = (
        P(COL, None, "row"),
        P("row", None, COL),
        P("row", COL),
        P(COL, "row"),
        P(None, COL, "row"),
        P(),
    )
    out_specs = P(ROW_COL, None)
    return jax.shard_map(local, mesh=torus, in_specs=in_specs, out_specs=out_specs, check_vma=False)
```

profile of v0, /device:TPU:1, one launch (start us, length us, event | category | flops | bytes accessed | tf_op | source)
XLA Modules:
  0.0 380.5 jit_solution(10519326108349929063)
XLA Ops:
  7.4 0.0 copy-start
  7.4 0.0 all-gather.2.cloned.1.call-start
  7.4 0.7 all-gather.2.cloned.1.call-update
  8.1 1.9 broadcast_in_dim.39
  9.9 9.0 %all-to-all-start = ((bf16[8,4,48,256]{3,2,1,0:T(8,128)(2,1)}), bf16[8,4,48,256]{3,2,1,0:T(8,128)(2,1)S(1)}, u32[]{:S(2)}, u32[]{:S(2)}) async-start(bf16[8,4,48,256]{3,2,1,0:T(8,128)(2,1)} %broadcast_in_dim.39), calls=%async_computation | async-start | bytes 1572864 | tf_op jit(solution)/shard_map/all_to_all | solution.py:13
  19.0 0.0 reduce-scatter.6.cloned.1.call-start
  19.0 0.8 convert_reduce_fusion
  19.8 0.8 select_reduce_fusion
  20.6 0.7 compare_and_fusion
  21.3 0.7 broadcast_clamp_fusion
  22.0 20.5 %all-to-all-done = bf16[8,4,48,256]{3,2,1,0:T(8,128)(2,1)S(1)} async-done(((bf16[8,4,48,256]{3,2,1,0:T(8,128)(2,1)}), bf16[8,4,48,256]{3,2,1,0:T(8,128)(2,1)S(1)}, u32[]{:S(2)}, u32[]{:S(2)}) %all-to-all-start) | async-done | bytes 786464 | tf_op jit(solution)/shard_map/all_to_all | solution.py:13
  42.5 3.9 %gather_fusion = bf16[1024,256]{1,0:T(8,128)(2,1)S(1)} fusion(bf16[1536,256]{1,0:T(8,128)(2,1)S(1)} %bitcast.24, s32[1024]{0:T(1024)S(1)} %broadcast_clamp_fusion), kind=kCustom, calls=%fused_computation | custom fusion | bytes 1052672 | tf_op jit(solution)/shard_map/jit(_take)/gather | solution.py:64
  46.5 0.0 copy-done
  46.5 0.8 fusion
  47.2 2.3 copy.14
  49.5 0.0 reduce-scatter.6.cloned.1.call-update
  49.5 29.5 %all-gather.2.cloned.1.call-done = bf16[32,48,3584]{2,1,0:T(8,128)(2,1)} async-done(((bf16[1,48,3584]{2,1,0:T(8,128)(2,1)}), bf16[32,48,3584]{2,1,0:T(8,128)(2,1)}) %all-gather.2.cloned.1.call-update) | async-done | bytes 11010064 | tf_op jit(solution)/shard_map/all_gather | solution.py:67
  79.1 17.0 %fusion.5 = f32[1536,896]{1,0:T(8,128)} fusion(bf16[1536,3584]{1,0:T(8,128)(2,1)} %bitcast.29, bf16[3584,896]{1,0:T(8,128)(2,1)} %param.8), kind=kOutput, calls=%fused_computation.19 | convolution fusion | flops 9865003008 | bytes 22937600 | tf_op jit(solution)/shard_map/dot_general | solution.py:69
  96.1 8.6 %gather_fusion.1 = f32[1024,896]{1,0:T(8,128)} fusion(f32[1536,896]{1,0:T(8,128)} %fusion.5, s32[1024]{0:T(1024)S(1)} %broadcast_clamp_fusion), kind=kCustom, calls=%fused_computation.1 | custom fusion | bytes 7344128 | tf_op jit(solution)/shard_map/jit(_take)/gather | solution.py:70
  104.7 4.2 %broadcast_select_fusion = f32[8,128,896]{2,1,0:T(8,128)} fusion(f32[8,128,896]{2,1,0:T(8,128)} %bitcast.27, pred[8,128]{1,0:T(8,128)(4,1)S(1)} %bitcast.28), kind=kLoop, calls=%fused_computation.4 | loop fusion | flops 917504 | bytes 7341056 | tf_op jit(solution)/shard_map/jit(_take)/select_n | solution.py:70
  108.9 6.7 %all-to-all-start.2 = ((f32[8,128,896]{2,1,0:T(8,128)}), f32[8,128,896]{2,1,0:T(8,128)}, u32[]{:S(2)}, u32[]{:S(2)}) async-start(f32[8,128,896]{2,1,0:T(8,128)} %broadcast_select_fusion), calls=%async_computation.3 | async-start | bytes 7340032 | tf_op jit(solution)/shard_map/all_to_all | solution.py:35
  115.6 0.0 reduce-scatter.8.cloned.1.call-start
  115.7 0.0 reduce-scatter.6.cloned.1.call-done
  115.7 0.5 reduce-scatter.8.cloned.1.call-update
  116.2 85.0 %all-to-all-done.2 = f32[8,128,896]{2,1,0:T(8,128)} async-done(((f32[8,128,896]{2,1,0:T(8,128)}), f32[8,128,896]{2,1,0:T(8,128)}, u32[]{:S(2)}, u32[]{:S(2)}) %all-to-all-start.2) | async-done | bytes 3670048 | tf_op jit(solution)/shard_map/all_to_all | solution.py:35
  201.2 2.2 reduce_sum.38
  203.5 0.2 copy.15
  203.7 1.5 broadcast_in_dim.46
  205.1 3.6 all-to-all-start.3
  208.7 0.0 reduce-scatter.8.cloned.1.call-done
  208.8 0.9 convert_bitcast_fusion
  209.7 42.1 %all-to-all-done.3 = bf16[8,128,896]{1,2,0:T(8,128)(2,1)S(1)} async-done(((bf16[8,128,896]{1,2,0:T(8,128)(2,1)}), bf16[8,128,896]{1,2,0:T(8,128)(2,1)S(1)}, u32[]{:S(2)}, u32[]{:S(2)}) %all-to-all-start.3) | async-done | bytes 1835040 | tf_op jit(solution)/shard_map/all_to_all | solution.py:13
  251.8 1.6 broadcast_in_dim.42
  253.4 8.6 %all-to-all-start.1 = ((bf16[32,32,1024]{2,1,0:T(8,128)(2,1)}), bf16[32,32,1024]{2,1,0:T(8,128)(2,1)}, u32[]{:S(2)}, u32[]{:S(2)}) async-start(bf16[32,32,1024]{2,1,0:T(8,128)(2,1)} %broadcast_in_dim.42), calls=%async_computation.2 | async-start | bytes 4194304 | tf_op jit(solution)/shard_map/all_to_all | solution.py:13
  262.0 2.7 copy.16
  264.7 3.6 bitcast_convert_fusion
  268.3 5.0 %copy.17 = f32[1024,896]{0,1:T(8,128)} copy(f32[1024,896]{1,0:T(8,128)} %bitcast_convert_fusion) | data formatting | bytes 7340032 | tf_op jit(solution)/shard_map/convert_element_type | solution.py:81
  273.3 16.6 %all-to-all-done.1 = bf16[32,32,1024]{2,1,0:T(8,128)(2,1)} async-done(((bf16[32,32,1024]{2,1,0:T(8,128)(2,1)}), bf16[32,32,1024]{2,1,0:T(8,128)(2,1)}, u32[]{:S(2)}, u32[]{:S(2)}) %all-to-all-start.1) | async-done | bytes 2097184 | tf_op jit(solution)/shard_map/all_to_all | solution.py:13
  289.9 0.0 copy-start.1
  289.9 7.8 %multiply_reduce_fusion = f32[1024,2]{0,1:T(2,128)S(1)} fusion(f32[1024,896]{0,1:T(8,128)} %copy.17, bf16[1024,1024,1]{1,0,2:T(8,128)(2,1)} %bitcast.6, bf16[2,896,1024]{2,1,0:T(8,128)(2,1)} %param.10), kind=kOutput, calls=%fused_computation.2 | convolution fusion | flops 3761764352 | bytes 9445376 | tf_op jit(solution)/shard_map/tj,qij->tqi/dot_general | solution.py:80
  297.8 74.6 %all-reduce.1 = f32[1024,2]{0,1:T(2,128)S(1)} all-reduce(f32[1024,2]{0,1:T(2,128)S(1)} %multiply_reduce_fusion), channel_id=4, replica_groups=mesh['row'=8,'col_0'=4,'col_1'=4,'col_2'=2] {'row','col_0','col_1','col_2'}, use_global_device_ids=true, to_apply=%region_6.7.clone | all-reduce | flops 2048 | bytes 16384
  372.4 0.6 constant_dynamic-slice_fusion
  373.0 0.0 copy-done.1
Async XLA Ops:
  7.4 39.1 %copy-start = (bf16[256,1024]{1,0:T(8,128)(2,1)S(1)}, bf16[256,1024]{1,0:T(8,128)(2,1)}, u32[]{:S(2)}) copy-start(bf16[256,1024]{1,0:T(8,128)(2,1)} %param.9) | copy-start | bytes 1572868
  7.4 71.7 %all-gather.2.cloned.1.call-start = ((), (), s32[]{:S(2)}) async-start(), calls=%async_computation.7 | async-start | bytes 11354112 | tf_op jit(solution)/shard_map/all_gather | solution.py:67
  9.9 32.6 %all-to-all-start = ((bf16[8,4,48,256]{3,2,1,0:T(8,128)(2,1)}), bf16[8,4,48,256]{3,2,1,0:T(8,128)(2,1)S(1)}, u32[]{:S(2)}, u32[]{:S(2)}) async-start(bf16[8,4,48,256]{3,2,1,0:T(8,128)(2,1)} %broadcast_in_dim.39), calls=%async_computation | async-start | bytes 1572864 | tf_op jit(solution)/shard_map/all_to_all | solution.py:13
  19.0 96.7 %reduce-scatter.6.cloned.1.call-start = ((), (), s32[]{:S(2)}) async-start(), calls=%async_computation.6 | async-start | bytes 6291456 | tf_op jit(solution)/shard_map/reduce_scatter | solution.py:44
  108.9 92.4 %all-to-all-start.2 = ((f32[8,128,896]{2,1,0:T(8,128)}), f32[8,128,896]{2,1,0:T(8,128)}, u32[]{:S(2)}, u32[]{:S(2)}) async-start(f32[8,128,896]{2,1,0:T(8,128)} %broadcast_select_fusion), calls=%async_computation.3 | async-start | bytes 7340032 | tf_op jit(solution)/shard_map/all_to_all | solution.py:35
  115.6 93.1 %reduce-scatter.8.cloned.1.call-start = ((), (), s32[]{:S(2)}) async-start(), calls=%async_computation.8 | async-start | bytes 2228224
  205.1 46.7 %all-to-all-start.3 = ((bf16[8,128,896]{1,2,0:T(8,128)(2,1)}), bf16[8,128,896]{1,2,0:T(8,128)(2,1)S(1)}, u32[]{:S(2)}, u32[]{:S(2)}) async-start(bf16[8,128,896]{1,2,0:T(8,128)(2,1)} %broadcast_in_dim.46), calls=%async_computation.4 | async-start | bytes 3670016 | tf_op jit(solution)/shard_map/all_to_all | solution.py:13
  253.4 36.5 %all-to-all-start.1 = ((bf16[32,32,1024]{2,1,0:T(8,128)(2,1)}), bf16[32,32,1024]{2,1,0:T(8,128)(2,1)}, u32[]{:S(2)}, u32[]{:S(2)}) async-start(bf16[32,32,1024]{2,1,0:T(8,128)(2,1)} %broadcast_in_dim.42), calls=%async_computation.2 | async-start | bytes 4194304 | tf_op jit(solution)/shard_map/all_to_all | solution.py:13
  289.9 83.1 %copy-start.1 = (bf16[256,1024]{1,0:T(8,128)(2,1)S(1)}, bf16[256,1024]{1,0:T(8,128)(2,1)}, u32[]{:S(2)}) copy-start(bf16[256,1024]{1,0:T(8,128)(2,1)} %param.9) | copy-start | bytes 1572868
Sparse Core Ops, SparseCore 0:
  10.7 68.2 all-gather.1
Sparse Core Ops, SparseCore 1:
  49.6 14.1 reduce-scatter.5
  120.1 77.6 reduce-scatter.7
where the time goes:
time: 381 us; the launch traced here: 380 us
  waiting for transfers between devices  195 us (51%)
  blocking collectives  74.6 us (20%)
  local copies, waits for them, and re-layouts  28.3 us (7%)
  starting transfers between devices  28 us (7%)
  matrix products  25.6 us (7%)
  between operations  14.9 us (4%)
  other arithmetic  13.8 us (4%)
    all_to_all x1, waiting for transfers between devices, summed_on_arrival(): lax.all_to_all(in_blocks(shard, dim, devices), axis, 0, 0, tiled=True)  85 us
    all_to_all x3, waiting for transfers between devices, copy_for_each(): return lax.all_to_all(copies, axis, split_axis=0, concat_axis=0, tiled=True)  79.3 us
    unnamed x1, blocking collectives  74.6 us
    all_gather x1, waiting for transfers between devices, local(): piece = lax.all_gather(out_grads, COL, axis=0, tiled=True)  29.5 us
    all_to_all x3, starting transfers between devices, copy_for_each(): return lax.all_to_all(copies, axis, split_axis=0, concat_axis=0, tiled=True)  21.2 us
    dot_general x1, matrix products, local(): slot_terms = jnp.dot(flattened, rot_out, preferred_element_type=jnp.float32)  17 us
    gather x1, local copies, waits for them, and re-layouts, local(): grad_terms = jnp.take(slot_terms, flat_index, axis=0)  8.63 us
    dot_general x1, matrix products, local(): jnp.einsum('tj,qij->tqi', rot_acts, queries, preferred_element_type=jnp.f...  7.84 us
  transfers between devices with their start and end apart: 7, of which 5 were waited for; matrix products, arithmetic and copies ran while one was open for 15% of the time, Pallas kernels for 0%

commit v1 on v0

v1 whole, which is shorter than its diff:
```python
import jax
import jax.numpy as jnp
from jax import lax
from jax.experimental import pallas as pl
from jax.experimental.pallas import tpu as pltpu
from jax.sharding import Mesh
from jax.sharding import PartitionSpec as P

COL = ("col_0", "col_1", "col_2")
ROW_COL = ("row", "col_0", "col_1", "col_2")
MESH = pl.DeviceIdType.MESH
F32 = jnp.float32
BF16 = jnp.bfloat16
I32 = jnp.int32

RING = 4
ZED = 8
SLOTS = 48
SEQS = 32
PART = 128
HALF = 64
OFFSETS = (0, -1, 1, 2)
N_SEMS = 192


def ring4(i):
    return lax.rem(i + 8, 4)


def ring8(i):
    return lax.rem(i + 16, 8)


def kernel(
    grads, acts, rot_out_hbm, rot_in_hbm, queries_hbm, tokens, out,
    gbuf, wout, win, wq, hilo, parts, arrivals, rot_grads, abuf, rap, pair_in,
    e1_half, e1_full, e2_half, e2_full, rot_acts, proj, hot, nat, rel, mine, zsum, plane,
    send_sems, recv_sems, local_sems,
):
    z = lax.axis_index("row")
    y = lax.axis_index("col_0")
    x = lax.axis_index("col_1")
    k = lax.axis_index("col_2")
    o = 1 - k
    p1 = x * o + y * k
    p2 = y * o + x * k
    dout = wout.shape[1]
    half_in = wout.shape[0] // 2

    def first(d):
        return (z, ring4(y + k * d), ring4(x + o * d), k)

    def second(d):
        return (z, ring4(y + o * d), ring4(x + k * d), k)

    def along_z(d):
        return (ring8(z + d), y, x, k)

    sibling = (z, y, x, o)

    def along_x(d):
        return (z, y, ring4(x + d), k)

    def along_y(d):
        return (z, ring4(y + d), x, k)

    peers = [sibling] + [along_z(d) for d in range(1, 8)]
    peers += [along_x(d) for d in (1, 2, 3)] + [along_y(d) for d in (1, 2, 3)]
    barrier = pltpu.get_barrier_semaphore()
    for peer in peers:
        pl.semaphore_signal(barrier, inc=1, device_id=peer, device_id_type=MESH)
    pl.semaphore_wait(barrier, len(peers))

    started = []
    ids = {}

    def sem_id(name):
        return ids.setdefault(name, len(ids))

    def send(name, src, dst, to):
        i = sem_id(name)
        copy = pltpu.make_async_remote_copy(
            src_ref=src, dst_ref=dst, send_sem=send_sems.at[i], recv_sem=recv_sems.at[i],
            device_id=to, device_id_type=MESH,
        )
        copy.start()
        started.append(copy)

    def arrived(name, dst):
        i = sem_id(name)
        pltpu.make_async_remote_copy(
            src_ref=dst, dst_ref=dst, send_sem=send_sems.at[i], recv_sem=recv_sems.at[i],
            device_id=sibling, device_id_type=MESH,
        ).wait_recv()

    lo, hi = pl.ds(0, half_in), pl.ds(half_in, half_in)

    def block(j, i):
        return gbuf.at[j, k * 4 + ring4(p1 + OFFSETS[i])]

    def sibling_block(j, i):
        return gbuf.at[j, o * 4 + ring4(p2 + OFFSETS[i])]

    own = grads.at[0]
    send("g1+", own, block(0, 0), first(1))
    send("g1-", own, block(0, 0), first(-1))
    send("a+1", acts, abuf.at[z], along_z(1))
    send("a-1", acts, abuf.at[z], along_z(-1))
    send("s00", own, block(0, 0), sibling)
    keep = pltpu.make_async_copy(own, block(0, 0), local_sems.at[0])
    keep_acts = pltpu.make_async_copy(acts, abuf.at[z], local_sems.at[1])
    load_in = pltpu.make_async_copy(rot_in_hbm, win, local_sems.at[2])
    load_out = pltpu.make_async_copy(rot_out_hbm, wout, local_sems.at[3])
    load_q = pltpu.make_async_copy(queries_hbm, wq, local_sems.at[4])
    for copy in (keep, keep_acts, load_in, load_out, load_q):
        copy.start()

    def token_rows():
        lane = lax.broadcasted_iota(I32, (PART, PART), 1)
        sub = lax.broadcasted_iota(I32, (PART, PART), 0)

        def count(t, starts):
            row = tokens[pl.ds(t, 1), :].astype(F32)
            col = jnp.broadcast_to(row, (PART, PART)).T.astype(I32)
            nat[t] = col
            return starts + jnp.sum(jnp.where(col < lane, 1.0, 0.0), axis=0, keepdims=True)

        starts = lax.fori_loop(0, ZED, count, jnp.zeros((1, PART), F32))

        def place(t, carry):
            col = nat[t]
            begin = jnp.sum(jnp.where(col == lane, starts, 0.0), axis=1, keepdims=True)
            slot = t * PART + sub - begin.astype(I32)
            nat[t] = col * SLOTS + slot
            core = col & 1
            cx = (col >> 1) & 3
            cy = col >> 3
            q1 = jnp.where(core == 0, cx, cy)
            dist = jnp.where(core == 0, cy - y, cx - x) & 3
            group = jnp.where(dist == 2, 3, jnp.where(dist == 3, 2, dist))
            rel[t] = (group * 8 + core * 4 + q1) * SLOTS + slot
            return carry

        lax.fori_loop(0, ZED, place, 0)

    def one_hot(where, t, row):
        col = where[t]
        lane = lax.broadcasted_iota(I32, (PART, PART), 1)
        for c in range(SEQS * SLOTS // PART):
            hot[row:row + PART, c * PART:(c + 1) * PART] = jnp.where(
                col == lane + c * PART, 1.0, 0.0
            ).astype(BF16)

    token_rows()

    def second_sends(i):
        send(f"h{i}+", block(0, i), block(2, i), second(1))
        send(f"h{i}-", block(0, i), block(1, i), second(-1))

    arrived("g1+", block(0, 1))
    send("g2+", block(0, 1).at[:, lo], block(0, 1).at[:, lo], first(1))
    arrived("g1-", block(0, 2))
    send("g2-", block(0, 2).at[:, hi], block(0, 2).at[:, hi], first(-1))
    keep.wait()
    second_sends(0)
    second_sends(1)
    second_sends(2)
    send("s01", block(0, 1), block(0, 1), sibling)
    send("s02", block(0, 2), block(0, 2), sibling)

    def z_hop(h):
        if h < 3:
            arrived(f"a+{h}", abuf.at[ring8(z - h)])
            send(f"a+{h + 1}", abuf.at[ring8(z - h)], abuf.at[ring8(z - h)], along_z(1))
            arrived(f"a-{h}", abuf.at[ring8(z + h)])
            send(f"a-{h + 1}", abuf.at[ring8(z + h)], abuf.at[ring8(z + h)], along_z(-1))
        else:
            a, b = pl.ds(0, 2), pl.ds(2, 2)
            arrived("a+3", abuf.at[ring8(z - 3)])
            send("a+4", abuf.at[ring8(z - 3), a], abuf.at[ring8(z - 3), a], along_z(1))
            arrived("a-3", abuf.at[ring8(z + 3)])
            send("a-4", abuf.at[ring8(z + 3), b], abuf.at[ring8(z + 3), b], along_z(-1))

    z_hop(1)
    z_hop(2)
    arrived("g2+", block(0, 3).at[:, lo])
    arrived("g2-", block(0, 3).at[:, hi])
    second_sends(3)
    send("s03", block(0, 3), block(0, 3), sibling)
    z_hop(3)

    def pass_on(i):
        arrived(f"h{i}+", block(2, i))
        send(f"i{i}+", block(2, i).at[:, lo], block(3, i).at[:, lo], second(1))
        arrived(f"h{i}-", block(1, i))
        send(f"i{i}-", block(1, i).at[:, hi], block(3, i).at[:, hi], second(-1))
        send(f"s1{i}", block(1, i), block(1, i), sibling)
        send(f"s2{i}", block(2, i), block(2, i), sibling)

    def opposite(i):
        arrived(f"i{i}+", block(3, i).at[:, lo])
        arrived(f"i{i}-", block(3, i).at[:, hi])
        send(f"s3{i}", block(3, i), block(3, i), sibling)

    def rotate_grads(j):
        rows = gbuf[j].reshape(8 * SLOTS, wout.shape[0])
        for n in range(0, dout, 256):
            width = min(256, dout - n)
            res = jnp.dot(rows, wout[:, n:n + width], preferred_element_type=F32)
            top = res.astype(BF16)
            hilo[j * 384:(j + 1) * 384, n:n + width] = top
            hilo[j * 384:(j + 1) * 384, dout + n:dout + n + width] = (
                res - top.astype(F32)
            ).astype(BF16)

    pass_on(0)
    for i in range(4):
        arrived(f"s0{i}", sibling_block(0, i))
    load_out.wait()
    rotate_grads(0)
    opposite(0)

    arrived("a+4", abuf.at[ring8(z + 4), pl.ds(0, 2)])
    arrived("a-4", abuf.at[ring8(z + 4), pl.ds(2, 2)])
    keep_acts.wait()
    load_in.wait()

    def rotate_acts(p):
        one_hot(nat, 2 * p, 0)
        one_hot(nat, 2 * p + 1, PART)
        slots = abuf[...].reshape(SEQS * SLOTS, abuf.shape[-1])
        rows = jnp.dot(hot[...], slots, preferred_element_type=F32).astype(BF16)
        res = jnp.dot(rows, win[...], preferred_element_type=F32)
        rap[pl.ds(p * 8, 8)] = res.reshape(8, 32, res.shape[-1])

    lax.fori_loop(0, 2, lambda n, c: (rotate_acts(o * 2 + n), c)[1], 0)
    send("pair", rap.at[pl.ds(o * 16, 16)], pair_in, sibling)
    pass_on(1)
    lax.fori_loop(0, 2, lambda n, c: (rotate_acts(k * 2 + n), c)[1], 0)
    opposite(1)
    pass_on(2)
    arrived("pair", pair_in)
    base = k * 16
    def add_pair(n, c):
        rap[base + n] += pair_in[n]
        return c
    lax.fori_loop(0, 16, add_pair, 0)
    opposite(2)
    pass_on(3)

    def quarter(d):
        return base + ring4(p1 + d) * 4

    send("e1+", rap.at[pl.ds(quarter(2), 2)], e1_half.at[0], first(1))
    send("e1-", rap.at[pl.ds(quarter(2) + 2, 2)], e1_half.at[1], first(-1))

    for j in (1, 2):
        for i in range(4):
            arrived(f"s{j}{i}", sibling_block(j, i))
        rotate_grads(j)
    opposite(3)

    def e1_second_step():
        arrived("e1+", e1_half.at[0])
        rap[pl.ds(quarter(1), 2)] += e1_half[0]
        send("e2+", rap.at[pl.ds(quarter(1), 4)], e1_full.at[0], first(1))
        arrived("e1-", e1_half.at[1])
        rap[pl.ds(quarter(-1) + 2, 2)] += e1_half[1]
        send("e2-", rap.at[pl.ds(quarter(-1), 4)], e1_full.at[1], first(-1))

    e1_second_step()
    for i in range(4):
        arrived(f"s3{i}", sibling_block(3, i))
    rotate_grads(3)

    def compact(ds):
        for n, d in enumerate(ds):
            one_hot(rel, ring8(z + d), n * PART)
        rows = len(ds) * PART
        for n in range(0, dout, 256):
            width = min(256, dout - n)
            res = jnp.dot(hot[:rows], hilo[:, n:n + width], preferred_element_type=F32)
            res += jnp.dot(
                hot[:rows], hilo[:, dout + n:dout + n + width], preferred_element_type=F32
            )
            for m, d in enumerate(ds):
                parts[ring8(z + d), :, n:n + width] = res[m * PART:(m + 1) * PART]

    A, B = pl.ds(0, HALF), pl.ds(HALF, HALF)

    def c_send(direction, h, part):
        s = 1 if direction == 0 else -1
        rows = parts.at[ring8(z + s * h), B if part else A]
        send(f"c{direction}{h}{part}", rows, arrivals.at[direction, 2 * (4 - h) + part], along_z(s))

    def c_take(direction, h, part):
        s = 1 if direction == 0 else -1
        slot = arrivals.at[direction, 2 * (3 - h) + part]
        arrived(f"c{direction}{h + 1}{part}", slot)
        rows = pl.ds(part * HALF, HALF)
        parts[ring8(z + s * h), rows, :] += arrivals[direction, 2 * (3 - h) + part]

    compact((4,))
    c_send(0, 4, 0)
    c_send(1, 4, 1)
    compact((3, -3))
    c_send(0, 3, 1)
    c_send(1, 3, 0)

    def hop(h, fresh):
        for direction in (0, 1):
            part = fresh if direction == 0 else 1 - fresh
            c_take(direction, h, part)
            c_send(direction, h, part)

    arrived("e2+", e1_full.at[0])
    arrived("e2-", e1_full.at[1])
    rap[pl.ds(quarter(0), 4)] += e1_full[0] + e1_full[1]
    mid = quarter(0)

    def eighth(d):
        return mid + ring4(p2 + d)

    top, low = pl.ds(0, 16), pl.ds(16, 16)
    send("f1+", rap.at[eighth(2), top], e2_half.at[0], second(1))
    send("f1-", rap.at[eighth(2), low], e2_half.at[1], second(-1))
    hop(3, 0)
    compact((2, -2))
    arrived("f1+", e2_half.at[0])
    rap[eighth(1), 0:16] += e2_half[0]
    send("f2+", rap.at[eighth(1)], e2_full.at[0], second(1))
    arrived("f1-", e2_half.at[1])
    rap[eighth(-1), 16:32] += e2_half[1]
    send("f2-", rap.at[eighth(-1)], e2_full.at[1], second(-1))
    hop(2, 1)
    arrived("f2+", e2_full.at[0])
    arrived("f2-", e2_full.at[1])
    rot_acts[eighth(0)] = (rap[eighth(0)] + e2_full[0] + e2_full[1]).astype(BF16)
    send("j1+", rot_acts.at[eighth(0)], rot_acts.at[eighth(0)], second(1))
    send("j1-", rot_acts.at[eighth(0)], rot_acts.at[eighth(0)], second(-1))
    compact((1, -1))
    hop(2, 0)
    arrived("j1+", rot_acts.at[eighth(-1)])
    send("j2+", rot_acts.at[eighth(-1), top], rot_acts.at[eighth(-1), top], second(1))
    arrived("j1-", rot_acts.at[eighth(1)])
    send("j2-", rot_acts.at[eighth(1), low], rot_acts.at[eighth(1), low], second(-1))
    compact((0,))
    arrived("j2+", rot_acts.at[eighth(2), top])
    arrived("j2-", rot_acts.at[eighth(2), low])

    def quarter_rows(d):
        return rot_acts.at[pl.ds(quarter(d), 4)]

    send("k1+", quarter_rows(0), quarter_rows(0), first(1))
    send("k1-", quarter_rows(0), quarter_rows(0), first(-1))
    send("t0", quarter_rows(0), quarter_rows(0), sibling)
    hop(1, 1)
    arrived("k1+", quarter_rows(-1))
    send("k2+", rot_acts.at[pl.ds(quarter(-1), 2)], rot_acts.at[pl.ds(quarter(-1), 2)], first(1))
    arrived("k1-", quarter_rows(1))
    send("k2-", rot_acts.at[pl.ds(quarter(1) + 2, 2)], rot_acts.at[pl.ds(quarter(1) + 2, 2)], first(-1))
    send("t1", quarter_rows(-1), quarter_rows(-1), sibling)
    send("t2", quarter_rows(1), quarter_rows(1), sibling)
    hop(1, 0)
    arrived("k2+", rot_acts.at[pl.ds(quarter(2), 2)])
    arrived("k2-", rot_acts.at[pl.ds(quarter(2) + 2, 2)])
    send("t3", quarter_rows(2), quarter_rows(2), sibling)
    for i, d in enumerate(OFFSETS):
        arrived(f"t{i}", rot_acts.at[pl.ds(o * 16 + ring4(p2 + d) * 4, 4)])
    load_q.wait()

    def project(t, carry):
        rows = rot_acts[pl.ds(t * 8, 8)].reshape(256, rot_acts.shape[-1])
        for q in range(2):
            res = lax.dot_general(
                rows, wq[q], (((1,), (1,)), ((), ())), preferred_element_type=F32
            )
            proj[pl.ds(2 * t, 2), q] = res.reshape(2, PART, dout)
        return carry

    lax.fori_loop(0, 4, project, 0)

    for part in (1, 0):
        rows = pl.ds(part * HALF, HALF)
        for direction in (0, 1):
            c_take(direction, 0, part)
        rot_grads[z, rows, :] = parts[z, rows, :].astype(BF16)
        for direction, s in ((0, 1), (1, -1)):
            ref = rot_grads.at[z, B if part else A]
            send(f"d{direction}1{part}", ref, ref, along_z(s))

    def score(t):
        tile = jnp.zeros((8, PART), F32)
        line = lax.broadcasted_iota(I32, (8, PART), 0)
        for q in range(2):
            total = jnp.zeros((PART, PART), F32)
            for n in range(0, dout, PART):
                total += rot_grads[t, :, n:n + PART].astype(F32) * proj[t, q, :, n:n + PART]
            sums = jnp.sum(total.T, axis=0, keepdims=True)
            tile = jnp.where(line == q, sums, tile)
        mine[t] = tile

    def give_score(d):
        t = ring8(z + d)
        score(t)
        send(f"z{d % 8}", mine.at[t], zsum.at[z], along_z(d))

    score(z)
    for h in (1, 2, 3):
        for part in (1, 0):
            for direction, s in ((0, 1), (1, -1)):
                ref = rot_grads.at[ring8(z - s * h), B if part else A]
                arrived(f"d{direction}{h}{part}", ref)
                if h < 3 or part == direction:
                    send(f"d{direction}{h + 1}{part}", ref, ref, along_z(s))
        give_score(-h)
        give_score(h)
    arrived("d040", rot_grads.at[ring8(z + 4), A])
    arrived("d141", rot_grads.at[ring8(z + 4), B])
    give_score(4)

    total = mine[z]
    for d in range(1, 8):
        src = ring8(z - d)
        arrived(f"z{d}", zsum.at[src])
        total += zsum[src]
    plane[0] = total
    send("core", plane.at[0], plane.at[1], sibling)
    arrived("core", plane.at[1])
    plane[2] = plane[0] + plane[1]
    for d in (1, 2, 3):
        send(f"x{d}", plane.at[2], plane.at[2 + d], along_x(d))
    for d in (1, 2, 3):
        arrived(f"x{d}", plane.at[2 + d])
    plane[6] = plane[2] + plane[3] + plane[4] + plane[5]
    for d in (1, 2, 3):
        send(f"y{d}", plane.at[6], plane.at[6 + d], along_y(d))
    for d in (1, 2, 3):
        arrived(f"y{d}", plane.at[6 + d])
    total = plane[6] + plane[7] + plane[8] + plane[9]
    c = (y * 4 + x) * 2 + k
    lane = lax.broadcasted_iota(I32, (8, PART), 1)
    line = lax.broadcasted_iota(I32, (8, PART), 0)
    pick = lane == c * 4 + line
    cols = [
        jnp.sum(jnp.where(pick, jnp.broadcast_to(total[q:q + 1], (8, PART)), 0.0), axis=1, keepdims=True)
        for q in range(2)
    ]
    both = jnp.where(lane == 0, cols[0], cols[1])
    out[...] = both[0:4, 0:2]

    for copy in started:
        copy.wait_send()
    assert len(ids) <= N_SEMS


def local(out_grads, acts, rot_out, rot_in, queries, token_sequence):
    din_r, dout_c = rot_out.shape
    din_c, din_z = rot_in.shape
    any_ref = pl.BlockSpec(memory_space=pl.ANY)
    vmem = pl.BlockSpec(memory_space=pltpu.VMEM)
    scratch = [
        pltpu.VMEM((4, 8, SLOTS, din_r), BF16),
        pltpu.VMEM((din_r, dout_c), BF16),
        pltpu.VMEM((din_c, din_z), BF16),
        pltpu.VMEM(queries.shape, BF16),
        pltpu.VMEM((SEQS * SLOTS, 2 * dout_c), BF16),
        pltpu.VMEM((ZED, PART, dout_c), F32),
        pltpu.VMEM((2, 8, HALF, dout_c), F32),
        pltpu.VMEM((ZED, PART, dout_c), BF16),
        pltpu.VMEM((ZED, 4, SLOTS, din_c), BF16),
        pltpu.VMEM((32, 32, din_z), F32),
        pltpu.VMEM((16, 32, din_z), F32),
        pltpu.VMEM((2, 2, 32, din_z), F32),
        pltpu.VMEM((2, 4, 32, din_z), F32),
        pltpu.VMEM((2, 16, din_z), F32),
        pltpu.VMEM((2, 32, din_z), F32),
        pltpu.VMEM((32, 32, din_z), BF16),
        pltpu.VMEM((ZED, 2, PART, dout_c), F32),
        pltpu.VMEM((2 * PART, SEQS * SLOTS), BF16),
        pltpu.VMEM((ZED, PART, PART), I32),
        pltpu.VMEM((ZED, PART, PART), I32),
        pltpu.VMEM((ZED, 8, PART), F32),
        pltpu.VMEM((ZED, 8, PART), F32),
        pltpu.VMEM((10, 8, PART), F32),
        pltpu.SemaphoreType.DMA((N_SEMS,)),
        pltpu.SemaphoreType.DMA((N_SEMS,)),
        pltpu.SemaphoreType.DMA((5,)),
    ]
    return pl.pallas_call(
        kernel,
        out_shape=jax.ShapeDtypeStruct((4, 2), F32),
        in_specs=[any_ref] * 5 + [vmem],
        out_specs=vmem,
        scratch_shapes=scratch,
        compiler_params=pltpu.CompilerParams(
            collective_id=0, has_side_effects=True, vmem_limit_bytes=62 * 1024 * 1024
        ),
        name="influence",
    )(out_grads, acts, rot_out, rot_in, queries, token_sequence.reshape(8, 128))


def solution(mesh):
    torus = Mesh(
        mesh.devices.reshape(mesh.shape["row"], 4, 4, 2), ("row", "col_0", "col_1", "col_2")
    )
    in_specs = (
        P(COL, None, "row"),
        P("row", None, COL),
        P("row", COL),
        P(COL, "row"),
        P(None, COL, "row"),
        P(),
    )
    out_specs = P(ROW_COL, None)
    return jax.shard_map(local, mesh=torus, in_specs=in_specs, out_specs=out_specs, check_vma=False)
```

time: 381 us -> 139 us (0.36)
  waiting for transfers between devices: 195 us -> 0 us
  Pallas kernels: 0 us -> 138 us
  blocking collectives: 74.6 us -> 0 us
  starting transfers between devices: 28 us -> 0 us
  local copies, waits for them, and re-layouts: 28.3 us -> 1.32 us
  matrix products: 25.6 us -> 0 us
  between operations: 14.9 us -> 0.01 us
  other arithmetic: 13.8 us -> 0 us
    all_to_all x4 -> x0, waiting for transfers between devices: 164 us -> none  [the longest x1 85 us: summed_on_arrival(): lax.all_to_all(in_blocks(shard, dim, devices), axis, 0, 0, tiled=True)]
    pallas_call x0 -> x1, Pallas kernels: none -> 138 us  [local(): pl.pallas_call(kernel, out_shape=jax.ShapeDtypeStruct((4, 2), F32), in_sp...]
    unnamed x1 -> x0, blocking collectives: 74.6 us -> none
    all_gather x1 -> x0, waiting for transfers between devices: 29.5 us -> none  [local(): piece = lax.all_gather(out_grads, COL, axis=0, tiled=True)]
    all_to_all x4 -> x0, starting transfers between devices: 28 us -> none  [the longest x3 21.2 us: copy_for_each(): return lax.all_to_all(copies, axis, split_axis=0, concat_axis=0, tiled=True)]
    dot_general x3 -> x0, matrix products: 25.6 us -> none  [the longest x1 17 us: local(): slot_terms = jnp.dot(flattened, rot_out, preferred_element_type=jnp.float32)]
    gather x2 -> x0, local copies, waits for them, and re-layouts: 12.6 us -> none  [the longest x1 8.63 us: local(): grad_terms = jnp.take(slot_terms, flat_index, axis=0)]
    convert_element_type x2 -> x0, local copies, waits for them, and re-layouts: 5.21 us -> none  [the longest x1 5.04 us: local(): score_terms = jnp.sum(projected * rot_grads[:, None, :], axis=2)]
  transfers between devices with their start and end apart: 7 -> 0, of which waited for: 5 -> 0; matrix products, arithmetic and copies ran while one was open for 15% -> 0% of each run, Pallas kernels for 0% -> 0%
where the time goes in v1:
time: 139 us
  Pallas kernels  138 us (99%)
    pallas_call x1, Pallas kernels, local(): pl.pallas_call(kernel, out_shape=jax.ShapeDtypeStruct((4, 2), F32), in_sp...  138 us

profile of v1, /device:TPU:1, one launch (start us, length us, event | category | flops | bytes accessed | tf_op | source)
XLA Modules:
  0.0 139.0 jit_solution(5508828452672095901)
XLA Ops:
  0.0 137.7 %influence.1 = f32[4,2]{1,0:T(4,128)} custom-call(bf16[1,48,3584]{2,1,0:T(8,128)(2,1)} %grads.1, bf16[4,48,256]{2,1,0:T(8,128)(2,1)} %acts.1, bf16[3584,896]{1,0:T(8,128)(2,1)} %rot_out_hbm.1, bf16[256,1024]{1,0:T(8,128)(2,1)} %rot_in_hbm.1, bf16[2,896,1024]{2,1,0:T(8,128)(2,1)} %queries_hbm.1, s32[8,128]{1,0:T(8,128)} %bitcast.1), custom_call_target="tpu_custom_call" | custom-call | tf_op jit(solution)/shard_map/influence/pallas_call | solution.py:490
  137.7 1.3 copy.7

commit v2 on v1

v2 whole, which is shorter than its diff:
```python
import jax
import jax.numpy as jnp
from jax import lax
from jax.experimental import pallas as pl
from jax.experimental.pallas import tpu as pltpu
from jax.sharding import Mesh
from jax.sharding import PartitionSpec as P

COL = ("col_0", "col_1", "col_2")
ROW_COL = ("row", "col_0", "col_1", "col_2")
MESH = pl.DeviceIdType.MESH
F32 = jnp.float32
BF16 = jnp.bfloat16
I32 = jnp.int32

RING = 4
ZED = 8
SLOTS = 48
SEQS = 32
PART = 128
HALF = 64
SUB = 32
OFFSETS = (0, -1, 1, 2)
OFFSETS2 = (0, 1, -1, 2)
PLACES = (
    (0, 0), (0, 1), (0, 2), (0, 3), (1, 0), (2, 0), (1, 1), (2, 1),
    (3, 0), (1, 2), (2, 2), (3, 1), (1, 3), (2, 3), (3, 2), (3, 3),
)
N_SEMS = 123
EARLY = 12 * 2 * SLOTS
LATE = 8 * SLOTS
KINDS = "gashicdepfjktzxy"


def ring4(i):
    return lax.rem(i + 8, 4)


def ring8(i):
    return lax.rem(i + 16, 8)


def kernel(
    grads, acts, rot_out_hbm, rot_in_hbm, queries_hbm, tokens, out,
    gbuf, wout, win, wq, hilo, parts, arrivals, rot_grads, abuf, rap, pair_in,
    e1_half, e1_full, e2_half, e2_full, rot_acts, proj, hot, order, nat, rel, perm, lanes, mine, zsum, plane,
    send_sems, recv_sems, local_sems,
):
    z = lax.axis_index("row")
    y = lax.axis_index("col_0")
    x = lax.axis_index("col_1")
    k = lax.axis_index("col_2")
    o = 1 - k
    p1 = x * o + y * k
    p2 = y * o + x * k
    dout = wout.shape[1]
    half_in = wout.shape[0] // 2

    def first(d):
        return (z, ring4(y + k * d), ring4(x + o * d), k)

    def second(d):
        return (z, ring4(y + o * d), ring4(x + k * d), k)

    def along_z(d):
        return (ring8(z + d), y, x, k)

    sibling = (z, y, x, o)

    def along_x(d):
        return (z, y, ring4(x + d), k)

    def along_y(d):
        return (z, ring4(y + d), x, k)

    peers = [sibling] + [along_z(d) for d in range(1, 8)]
    peers += [along_x(d) for d in (1, 2, 3)] + [along_y(d) for d in (1, 2, 3)]
    barrier = pltpu.get_barrier_semaphore()
    for peer in peers:
        pl.semaphore_signal(barrier, inc=1, device_id=peer, device_id_type=MESH)

    ids = {}

    def sem_id(name):
        return ids.setdefault(name, len(ids))

    def send(name, src, dst, to):
        kind = KINDS.index(name[0])
        pltpu.make_async_remote_copy(
            src_ref=src, dst_ref=dst, send_sem=send_sems.at[kind],
            recv_sem=recv_sems.at[sem_id(name)], device_id=to, device_id_type=MESH,
        ).start()

    def sent(kind, ref):
        pltpu.make_async_remote_copy(
            src_ref=ref, dst_ref=ref, send_sem=send_sems.at[KINDS.index(kind)],
            recv_sem=recv_sems.at[0], device_id=sibling, device_id_type=MESH,
        ).wait_send()

    def arrived(name, dst):
        i = sem_id(name)
        pltpu.make_async_remote_copy(
            src_ref=dst, dst_ref=dst, send_sem=send_sems.at[0], recv_sem=recv_sems.at[i],
            device_id=sibling, device_id_type=MESH,
        ).wait_recv()

    lo, hi = pl.ds(0, half_in), pl.ds(half_in, half_in)

    def block(j, i):
        return gbuf.at[PLACES.index((j, i)), k]

    def sibling_block(j, i):
        return gbuf.at[PLACES.index((j, i)), o]

    own = grads.at[0]
    keep = pltpu.make_async_copy(own, block(0, 0), local_sems.at[0])
    keep_acts = pltpu.make_async_copy(acts, abuf.at[z], local_sems.at[1])
    load_in = pltpu.make_async_copy(rot_in_hbm, win, local_sems.at[2])
    load_out = pltpu.make_async_copy(rot_out_hbm, wout, local_sems.at[3])
    load_q = pltpu.make_async_copy(queries_hbm, wq, local_sems.at[4])
    for copy in (keep, keep_acts, load_in, load_out, load_q):
        copy.start()

    def token_rows():
        lane = lax.broadcasted_iota(I32, (PART, PART), 1)
        sub = lax.broadcasted_iota(I32, (PART, PART), 0)

        def place_of(core, seq_y, seq_x):
            near = jnp.where(core == 0, seq_x - x, seq_y - y) & 3
            far = jnp.where(core == 0, seq_y - y, seq_x - x) & 3
            where = far * 4 + near
            at = jnp.zeros_like(where)
            for place, (j, i) in enumerate(PLACES):
                at = jnp.where(where == (OFFSETS2[j] % 4) * 4 + OFFSETS[i] % 4, place, at)
            return at * 2 + core

        head = lax.broadcasted_iota(I32, (8, PART), 1)
        core, at = head & 1, head >> 1
        near, far = jnp.zeros_like(at), jnp.zeros_like(at)
        for place, (j, i) in enumerate(PLACES):
            near = jnp.where(at == place, OFFSETS[i], near)
            far = jnp.where(at == place, OFFSETS2[j], far)
        seq_x = jnp.where(core == 0, near, far) + x
        seq_y = jnp.where(core == 0, far, near) + y
        held = ((seq_y & 3) * 8 + (seq_x & 3) * 2 + core)[0:1]

        def count(t, sums):
            row = tokens[pl.ds(t, 1), :].astype(F32)
            col = jnp.broadcast_to(row, (PART, PART)).T.astype(I32)
            nat[t] = col
            rank = place_of(col & 1, col >> 3, (col >> 1) & 3)
            return tuple(
                old + jnp.sum(jnp.where(mark, 1.0, 0.0), axis=0, keepdims=True)
                for old, mark in zip(sums, (col < lane, rank < lane, col < held))
            )

        zero = jnp.zeros((1, PART), F32)
        begins, ranked, origin = lax.fori_loop(0, ZED, count, (zero, zero, zero))

        def place(t, carry):
            col = nat[t]
            begin = jnp.sum(jnp.where(col == lane, begins, 0.0), axis=1, keepdims=True)
            nat[t] = col * SLOTS + t * PART + sub - begin.astype(I32)
            u = (sub >> 6) * 512 + t * HALF + (sub & (HALF - 1))
            before = ranked <= u.astype(F32)
            rank = jnp.sum(jnp.where(before, 1.0, 0.0), axis=1, keepdims=True) - 1.0
            start = jnp.max(jnp.where(before, ranked, 0.0), axis=1, keepdims=True)
            first_of = jnp.sum(
                jnp.where(lane.astype(F32) == rank, origin, 0.0), axis=1, keepdims=True
            )
            slot = u - start.astype(I32)
            rel[t] = rank.astype(I32) * SLOTS + slot
            perm[t] = first_of.astype(I32) + slot
            return carry

        lax.fori_loop(0, ZED, place, 0)

    def one_hot(target, row, where, low, high):
        count = where.shape[0]
        lane = lax.broadcasted_iota(I32, (count, PART), 1)
        for c in range(low // PART, high // PART):
            target[row:row + count, c * PART:(c + 1) * PART] = jnp.where(
                where == lane + c * PART, 1.0, 0.0
            ).astype(BF16)

    token_rows()

    pl.semaphore_wait(barrier, len(peers))

    send("g1+", own, block(0, 1), first(1))
    send("g1-", own, block(0, 2), first(-1))
    send("s00", own, block(0, 0), sibling)
    send("a+1", acts, abuf.at[z], along_z(1))
    send("a-1", acts, abuf.at[z], along_z(-1))

    def second_sends(i, src=None):
        src = block(0, i) if src is None else src
        send(f"h{i}+", src, block(2, i), second(1))
        send(f"h{i}-", src, block(1, i), second(-1))

    def z_hop(h):
        for sign, s, part in (("+", 1, 0), ("-", -1, 2)):
            ref = abuf.at[ring8(z - s * h)]
            arrived(f"a{sign}{h}", ref)
            ref = ref if h < 3 else ref.at[pl.ds(part, 2)]
            send(f"a{sign}{h + 1}", ref, ref, along_z(s))

    def pass_on(i):
        arrived(f"h{i}+", block(2, i))
        send(f"i{i}+", block(2, i).at[:, lo], block(3, i).at[:, lo], second(1))
        arrived(f"h{i}-", block(1, i))
        send(f"i{i}-", block(1, i).at[:, hi], block(3, i).at[:, hi], second(-1))
        send(f"s1{i}", block(1, i), block(1, i), sibling)
        send(f"s2{i}", block(2, i), block(2, i), sibling)

    def opposite(i):
        arrived(f"i{i}+", block(3, i).at[:, lo])
        arrived(f"i{i}-", block(3, i).at[:, hi])
        send(f"s3{i}", block(3, i), block(3, i), sibling)

    def rotate_grads(start, stop):
        for j, i in PLACES[start:stop]:
            arrived(f"s{j}{i}", sibling_block(j, i))
        rows = gbuf[start:stop].reshape((stop - start) * 2 * SLOTS, wout.shape[0])
        at = slice(start * 2 * SLOTS, stop * 2 * SLOTS)
        for n in range(0, dout, 256):
            width = min(256, dout - n)
            res = jnp.dot(rows, wout[:, n:n + width], preferred_element_type=F32)
            top = res.astype(BF16)
            hilo[at, n:n + width] = top
            hilo[at, dout + n:dout + n + width] = (res - top.astype(F32)).astype(BF16)

    def rotate_acts(p):
        one_hot(hot, 0, nat[2 * p], 0, SEQS * SLOTS)
        one_hot(hot, PART, nat[2 * p + 1], 0, SEQS * SLOTS)
        slots = abuf[...].reshape(SEQS * SLOTS, abuf.shape[-1])
        rows = jnp.dot(hot[:2 * PART], slots, preferred_element_type=F32).astype(BF16)
        res = jnp.dot(rows, win[...], preferred_element_type=F32)
        rap[pl.ds(p * 8, 8)] = res.reshape(8, 32, res.shape[-1])

    second_sends(0, own)
    arrived("g1+", block(0, 1))
    send("g2+", block(0, 1).at[:, lo], block(0, 3).at[:, lo], first(1))
    arrived("g1-", block(0, 2))
    send("g2-", block(0, 2).at[:, hi], block(0, 3).at[:, hi], first(-1))
    second_sends(1)
    second_sends(2)
    send("s01", block(0, 1), block(0, 1), sibling)
    send("s02", block(0, 2), block(0, 2), sibling)
    z_hop(1)
    keep.wait()
    load_out.wait()
    pass_on(0)
    z_hop(2)
    arrived("g2+", block(0, 3).at[:, lo])
    arrived("g2-", block(0, 3).at[:, hi])
    second_sends(3)
    send("s03", block(0, 3), block(0, 3), sibling)
    def compact(ds, half):
        low, high = (0, EARLY) if half == 0 else (LATE, SEQS * SLOTS)
        rows = slice(half * HALF, (half + 1) * HALF)
        for n, d in enumerate(ds):
            one_hot(hot, n * HALF, rel[ring8(z + d), rows], low, high)
        picks = hot[:len(ds) * HALF, low:high]
        for n in range(0, dout, 256):
            width = min(256, dout - n)
            res = jnp.dot(picks, hilo[low:high, n:n + width], preferred_element_type=F32)
            res += jnp.dot(
                picks, hilo[low:high, dout + n:dout + n + width], preferred_element_type=F32
            )
            for m, d in enumerate(ds):
                parts[ring8(z + d), rows, n:n + width] = res[m * HALF:(m + 1) * HALF]

    SIGNS = (1, -1)

    def c_send(half, direction, h, sub):
        s = SIGNS[direction]
        rows = parts.at[ring8(z + s * h), pl.ds(half * HALF + sub * SUB, SUB)]
        slot = arrivals.at[half, direction, 2 * (4 - h) + sub]
        send(f"c{half}{direction}{h}{sub}", rows, slot, along_z(s))

    def c_take(half, direction, h, sub):
        s = SIGNS[direction]
        at = 2 * (3 - h) + sub
        arrived(f"c{half}{direction}{h + 1}{sub}", arrivals.at[half, direction, at])
        rows = pl.ds(half * HALF + sub * SUB, SUB)
        parts[ring8(z + s * h), rows, :] += arrivals[half, direction, at]

    def c_open(half):
        c_send(half, 0, 4, 0)
        c_send(half, 1, 4, 1)
        c_send(half, 0, 3, 1)
        c_send(half, 1, 3, 0)

    def hop(half, h, fresh):
        for direction in (0, 1):
            sub = fresh if direction == 0 else 1 - fresh
            c_take(half, direction, h, sub)
            c_send(half, direction, h, sub)

    def d_ref(half, d):
        return rot_grads.at[ring8(z + d), pl.ds(half * HALF, HALF)]

    def c_close(half):
        for sub in (1, 0):
            for direction in (0, 1):
                c_take(half, direction, 0, sub)
        rows = pl.ds(half * HALF, HALF)
        rot_grads[z, rows, :] = parts[z, rows, :].astype(BF16)
        for direction, s in enumerate(SIGNS):
            send(f"d{half}{direction}1", d_ref(half, 0), d_ref(half, 0), along_z(s))

    def d_hop(half, h):
        for direction, s in enumerate(SIGNS):
            ref = d_ref(half, -s * h)
            if h < 4:
                arrived(f"d{half}{direction}{h}", ref)
            if h == 3:
                ref = ref.at[pl.ds(direction * SUB, SUB)]
            if h == 4:
                ref = ref.at[pl.ds(direction * SUB, SUB)]
                arrived(f"d{half}{direction}{h}", ref)
            else:
                send(f"d{half}{direction}{h + 1}", ref, ref, along_z(s))

    rotate_grads(0, 3)
    z_hop(3)
    pass_on(1)
    opposite(0)
    arrived("a+4", abuf.at[ring8(z + 4), pl.ds(0, 2)])
    arrived("a-4", abuf.at[ring8(z + 4), pl.ds(2, 2)])
    keep_acts.wait()
    load_in.wait()
    lax.fori_loop(0, 2, lambda n, c: (rotate_acts(o * 2 + n), c)[1], 0)
    send("pair", rap.at[pl.ds(o * 16, 16)], pair_in, sibling)
    rotate_grads(3, 8)
    pass_on(2)
    opposite(1)
    rotate_grads(8, 12)
    compact((4, 3, -3), 0)
    c_open(0)
    pass_on(3)
    opposite(2)
    compact((2, -2, 1, -1, 0), 0)
    hop(0, 3, 0)
    lax.fori_loop(0, 2, lambda n, c: (rotate_acts(k * 2 + n), c)[1], 0)
    arrived("pair", pair_in)
    base = k * 16

    def add_pair(n, c):
        rap[base + n] += pair_in[n]
        return c

    lax.fori_loop(0, 16, add_pair, 0)

    def quarter(d):
        return base + ring4(p1 + d) * 4

    send("e1+", rap.at[pl.ds(quarter(2), 2)], e1_half.at[0], first(1))
    send("e1-", rap.at[pl.ds(quarter(2) + 2, 2)], e1_half.at[1], first(-1))
    hop(0, 2, 1)
    opposite(3)
    rotate_grads(12, 15)
    hop(0, 2, 0)
    arrived("e1+", e1_half.at[0])
    rap[pl.ds(quarter(1), 2)] += e1_half[0]
    send("e2+", rap.at[pl.ds(quarter(1), 4)], e1_full.at[0], first(1))
    arrived("e1-", e1_half.at[1])
    rap[pl.ds(quarter(-1) + 2, 2)] += e1_half[1]
    send("e2-", rap.at[pl.ds(quarter(-1), 4)], e1_full.at[1], first(-1))
    rotate_grads(15, 16)
    hop(0, 1, 1)
    compact((4, 3, -3), 1)
    c_open(1)
    hop(0, 1, 0)
    arrived("e2+", e1_full.at[0])
    arrived("e2-", e1_full.at[1])
    rap[pl.ds(quarter(0), 4)] += e1_full[0] + e1_full[1]
    mid = quarter(0)

    def eighth(d):
        return mid + ring4(p2 + d)

    top, low = pl.ds(0, 16), pl.ds(16, 16)
    send("f1+", rap.at[eighth(2), top], e2_half.at[0], second(1))
    send("f1-", rap.at[eighth(2), low], e2_half.at[1], second(-1))
    compact((2, -2, 1, -1, 0), 1)
    hop(1, 3, 0)
    c_close(0)
    arrived("f1+", e2_half.at[0])
    rap[eighth(1), 0:16] += e2_half[0]
    send("f2+", rap.at[eighth(1)], e2_full.at[0], second(1))
    arrived("f1-", e2_half.at[1])
    rap[eighth(-1), 16:32] += e2_half[1]
    send("f2-", rap.at[eighth(-1)], e2_full.at[1], second(-1))
    hop(1, 2, 1)
    arrived("f2+", e2_full.at[0])
    arrived("f2-", e2_full.at[1])
    rot_acts[eighth(0)] = (rap[eighth(0)] + e2_full[0] + e2_full[1]).astype(BF16)
    send("j1+", rot_acts.at[eighth(0)], rot_acts.at[eighth(0)], second(1))
    send("j1-", rot_acts.at[eighth(0)], rot_acts.at[eighth(0)], second(-1))

    def fill_order(t, carry):
        one_hot(order.at[t], 0, perm[t], 0, ZED * PART)
        return carry

    lax.fori_loop(0, ZED, fill_order, 0)
    hop(1, 2, 0)
    d_hop(0, 1)
    arrived("j1+", rot_acts.at[eighth(-1)])
    send("j2+", rot_acts.at[eighth(-1), top], rot_acts.at[eighth(-1), top], second(1))
    arrived("j1-", rot_acts.at[eighth(1)])
    send("j2-", rot_acts.at[eighth(1), low], rot_acts.at[eighth(1), low], second(-1))
    hop(1, 1, 1)
    arrived("j2+", rot_acts.at[eighth(2), top])
    arrived("j2-", rot_acts.at[eighth(2), low])

    def quarter_rows(d):
        return rot_acts.at[pl.ds(quarter(d), 4)]

    send("k1+", quarter_rows(0), quarter_rows(0), first(1))
    send("k1-", quarter_rows(0), quarter_rows(0), first(-1))
    send("t0", quarter_rows(0), quarter_rows(0), sibling)
    hop(1, 1, 0)
    d_hop(0, 2)
    arrived("k1+", quarter_rows(-1))
    ref = rot_acts.at[pl.ds(quarter(-1), 2)]
    send("k2+", ref, ref, first(1))
    arrived("k1-", quarter_rows(1))
    ref = rot_acts.at[pl.ds(quarter(1) + 2, 2)]
    send("k2-", ref, ref, first(-1))
    send("t1", quarter_rows(-1), quarter_rows(-1), sibling)
    send("t2", quarter_rows(1), quarter_rows(1), sibling)
    c_close(1)
    d_hop(0, 3)
    arrived("k2+", rot_acts.at[pl.ds(quarter(2), 2)])
    arrived("k2-", rot_acts.at[pl.ds(quarter(2) + 2, 2)])
    send("t3", quarter_rows(2), quarter_rows(2), sibling)
    for i, d in enumerate(OFFSETS):
        arrived(f"t{i}", rot_acts.at[pl.ds(o * 16 + ring4(p2 + d) * 4, 4)])
    load_q.wait()

    def project(t):
        own_order = order[2 * t:2 * t + 2].reshape(2 * PART, ZED * PART)
        natural = rot_acts[...].reshape(ZED * PART, rot_acts.shape[-1])
        rows = jnp.dot(own_order, natural, preferred_element_type=F32).astype(BF16)
        for q in range(2):
            res = lax.dot_general(
                rows, wq[q], (((1,), (1,)), ((), ())), preferred_element_type=F32
            )
            proj[2 * t:2 * t + 2, q] = res.reshape(2, PART, dout)

    def multiply(t, half):
        rows = pl.ds(half * HALF, HALF)
        for q in range(2):
            total = jnp.zeros((HALF, PART), F32)
            for n in range(0, dout, PART):
                total += (
                    rot_grads[t, rows, n:n + PART].astype(F32) * proj[t, q, rows, n:n + PART]
                )
            lanes[t, q, rows, :] = total

    line = lax.broadcasted_iota(I32, (16, PART), 0)

    def in_token_order(t):
        tile = jnp.zeros((16, PART), F32)
        for q in range(2):
            rest = jnp.sum(lanes[t, q].T, axis=0, keepdims=True)
            for term in range(3):
                piece = rest.astype(BF16).astype(F32)
                tile = jnp.where(line == 2 * term + q, piece, tile)
                rest = rest - piece
        return jnp.dot(tile.astype(BF16), order[t], preferred_element_type=F32)

    project(0)
    project(1)
    d_hop(1, 1)
    project(2)
    d_hop(0, 4)
    project(3)
    d_hop(1, 2)

    def multiply_early(t, carry):
        multiply(t, 0)
        return carry

    lax.fori_loop(0, ZED, multiply_early, 0)
    multiply(z, 1)
    scores = in_token_order(z)
    for d in (1, -1, 2, -2):
        multiply(ring8(z + d), 1)
        scores += in_token_order(ring8(z + d))
    d_hop(1, 3)
    for d in (3, -3):
        multiply(ring8(z + d), 1)
        scores += in_token_order(ring8(z + d))
    d_hop(1, 4)
    multiply(ring8(z + 4), 1)
    scores += in_token_order(ring8(z + 4))
    scores = scores[0:8] + jnp.where(
        lax.broadcasted_iota(I32, scores[0:8].shape, 0) < 2,
        pltpu.roll(scores[0:8], 6, 0) + pltpu.roll(scores[0:8], 4, 0), 0.0
    )
    for t in range(ZED):
        mine[t] = scores[:, t * PART:(t + 1) * PART]
    for d in range(1, 8):
        send(f"z{d}", mine.at[ring8(z + d)], zsum.at[z], along_z(d))
    total = mine[z]
    for d in range(1, 8):
        src = ring8(z - d)
        arrived(f"z{d}", zsum.at[src])
        total += zsum[src]
    plane[0] = total
    send("xcore", plane.at[0], plane.at[1], sibling)
    arrived("xcore", plane.at[1])
    plane[2] = plane[0] + plane[1]
    for d in (1, 2, 3):
        send(f"x{d}", plane.at[2], plane.at[2 + d], along_x(d))
    for d in (1, 2, 3):
        arrived(f"x{d}", plane.at[2 + d])
    plane[6] = plane[2] + plane[3] + plane[4] + plane[5]
    for d in (1, 2, 3):
        send(f"y{d}", plane.at[6], plane.at[6 + d], along_y(d))
    for d in (1, 2, 3):
        arrived(f"y{d}", plane.at[6 + d])
    total = plane[6] + plane[7] + plane[8] + plane[9]
    c = (y * 4 + x) * 2 + k
    lane = lax.broadcasted_iota(I32, (8, PART), 1)
    row = lax.broadcasted_iota(I32, (8, PART), 0)
    pick = lane == c * 4 + row
    cols = [
        jnp.sum(
            jnp.where(pick, jnp.broadcast_to(total[q:q + 1], (8, PART)), 0.0),
            axis=1, keepdims=True,
        )
        for q in range(2)
    ]
    both = jnp.where(lane == 0, cols[0], cols[1])
    out[...] = both[0:4, 0:2]

    sent("g", gbuf.at[pl.ds(0, 3), 0])
    sent("a", abuf.at[pl.ds(0, 7)])
    sent("s", gbuf.at[pl.ds(0, 8)])
    sent("h", gbuf.at[pl.ds(0, 4)])
    sent("i", gbuf.at[pl.ds(0, 2)])
    sent("c", parts.at[pl.ds(0, 7)])
    sent("d", rot_grads.at[pl.ds(0, 7)])
    sent("e", rap.at[pl.ds(0, 12)])
    sent("p", pair_in)
    sent("f", rap.at[pl.ds(0, 3)])
    sent("j", rot_acts.at[pl.ds(0, 3)])
    sent("k", rot_acts.at[pl.ds(0, 12)])
    sent("t", rot_acts.at[pl.ds(0, 16)])
    sent("z", zsum.at[pl.ds(0, 7)])
    sent("x", plane.at[pl.ds(0, 4)])
    sent("y", plane.at[pl.ds(0, 3)])
    assert len(ids) == N_SEMS


def local(out_grads, acts, rot_out, rot_in, queries, token_sequence):
    din_r, dout_c = rot_out.shape
    din_c, din_z = rot_in.shape
    any_ref = pl.BlockSpec(memory_space=pl.ANY)
    vmem = pl.BlockSpec(memory_space=pltpu.VMEM)
    scratch = [
        pltpu.VMEM((16, 2, SLOTS, din_r), BF16),
        pltpu.VMEM((din_r, dout_c), BF16),
        pltpu.VMEM((din_c, din_z), BF16),
        pltpu.VMEM(queries.shape, BF16),
        pltpu.VMEM((SEQS * SLOTS, 2 * dout_c), BF16),
        pltpu.VMEM((ZED, PART, dout_c), F32),
        pltpu.VMEM((2, 2, 8, SUB, dout_c), F32),
        pltpu.VMEM((ZED, PART, dout_c), BF16),
        pltpu.VMEM((ZED, 4, SLOTS, din_c), BF16),
        pltpu.VMEM((32, 32, din_z), F32),
        pltpu.VMEM((16, 32, din_z), F32),
        pltpu.VMEM((2, 2, 32, din_z), F32),
        pltpu.VMEM((2, 4, 32, din_z), F32),
        pltpu.VMEM((2, 16, din_z), F32),
        pltpu.VMEM((2, 32, din_z), F32),
        pltpu.VMEM((32, 32, din_z), BF16),
        pltpu.VMEM((ZED, 2, PART, dout_c), F32),
        pltpu.VMEM((5 * HALF, SEQS * SLOTS), BF16),
        pltpu.VMEM((ZED, PART, ZED * PART), BF16),
        pltpu.VMEM((ZED, PART, PART), I32),
        pltpu.VMEM((ZED, PART, PART), I32),
        pltpu.VMEM((ZED, PART, PART), I32),
        pltpu.VMEM((ZED, 2, PART, PART), F32),
        pltpu.VMEM((ZED, 8, PART), F32),
        pltpu.VMEM((ZED, 8, PART), F32),
        pltpu.VMEM((10, 8, PART), F32),
        pltpu.SemaphoreType.DMA((len(KINDS),)),
        pltpu.SemaphoreType.DMA((N_SEMS,)),
        pltpu.SemaphoreType.DMA((5,)),
    ]
    return pl.pallas_call(
        kernel,
        out_shape=jax.ShapeDtypeStruct((4, 2), F32),
        in_specs=[any_ref] * 5 + [vmem],
        out_specs=vmem,
        scratch_shapes=scratch,
        compiler_params=pltpu.CompilerParams(
            collective_id=0, has_side_effects=True, vmem_limit_bytes=62 * 1024 * 1024
        ),
        name="influence",
    )(out_grads, acts, rot_out, rot_in, queries, token_sequence.reshape(8, 128))


def solution(mesh):
    torus = Mesh(
        mesh.devices.reshape(mesh.shape["row"], 4, 4, 2), ("row", "col_0", "col_1", "col_2")
    )
    in_specs = (
        P(COL, None, "row"),
        P("row", None, COL),
        P("row", COL),
        P(COL, "row"),
        P(None, COL, "row"),
        P(),
    )
    out_specs = P(ROW_COL, None)
    return jax.shard_map(local, mesh=torus, in_specs=in_specs, out_specs=out_specs, check_vma=False)
```

time: 139 us -> 126 us (0.906)
  Pallas kernels: 138 us -> 125 us
    pallas_call x1, Pallas kernels: 138 us -> 125 us  [local(): pl.pallas_call(kernel, out_shape=jax.ShapeDtypeStruct((4, 2), F32), in_sp...]
where the time goes in v2:
time: 126 us
  Pallas kernels  125 us (99%)
  local copies, waits for them, and re-layouts  1.32 us (1%)
    pallas_call x1, Pallas kernels, local(): pl.pallas_call(kernel, out_shape=jax.ShapeDtypeStruct((4, 2), F32), in_sp...  125 us

profile of v2, /device:TPU:1, one launch (start us, length us, event | category | flops | bytes accessed | tf_op | source)
XLA Modules:
  0.0 126.3 jit_solution(9671351905565285974)
XLA Ops:
  0.0 124.9 %influence.1 = f32[4,2]{1,0:T(4,128)} custom-call(bf16[1,48,3584]{2,1,0:T(8,128)(2,1)} %grads.1, bf16[4,48,256]{2,1,0:T(8,128)(2,1)} %acts.1, bf16[3584,896]{1,0:T(8,128)(2,1)} %rot_out_hbm.1, bf16[256,1024]{1,0:T(8,128)(2,1)} %rot_in_hbm.1, bf16[2,896,1024]{2,1,0:T(8,128)(2,1)} %queries_hbm.1, s32[8,128]{1,0:T(8,128)} %bitcast.1), custom_call_target="tpu_custom_call" | custom-call | tf_op jit(solution)/shard_map/influence/pallas_call | solution.py:596
  124.9 1.3 %copy.7 = f32[4,2]{0,1:T(2,128)} copy(f32[4,2]{1,0:T(4,128)} %influence.1) | data formatting | bytes 64 | tf_op jit(solution)/shard_map/influence/pallas_call | solution.py:596
